TPU v7x, 32 devices: a whole 2x2x4 slice. The times are simulated.
32 devices in a mesh: wide: 8 (over z, core), narrow: 4 (over y, x).
Axes of the slice: x: 2, y: 2, z: 4, core: 2. Of those that a mesh axis runs over, the one named last changes fastest.
Arguments:
- cholesky: bfloat16 [2048, 262144], P('narrow', 'wide'), may hold values from -0.015625 to 0.015625
- fields: bfloat16 [2, 32, 2048], P(None, 'wide', 'narrow'), may hold values from -4 to 4
- walkers: bfloat16 [32, 512, 128], P(('wide', 'narrow')), may hold values from -5 to 5
- one_body: bfloat16 [512, 512], replicated, may hold values from -0.078125 to 1
Outputs:
- propagated: bfloat16 [32, 512, 128], P(('wide', 'narrow'))
All inputs are finite; a program needn't handle non-finite values.
Results may differ from a plain program's by a relative error of at most 0.024.
Values may be sent and summed in bfloat16 or wider, within the bound.
A program may use at most 128 MiB of HBM per device.

v0:
```python
import jax
import jax.numpy as jnp
from jax import lax
from jax.sharding import PartitionSpec as P

ORDER = 6


def rotation_table(columns):
    half_cols = columns // 2
    source = lax.broadcasted_iota(jnp.int32, (columns, columns), 0)
    target = lax.broadcasted_iota(jnp.int32, (columns, columns), 1)
    negative = jnp.where((target < half_cols) & (source == target + half_cols), -1.0, 0.0)
    positive = jnp.where((target >= half_cols) & (source == target - half_cols), 1.0, 0.0)
    return (negative + positive).astype(jnp.bfloat16)


def advance(propagator, current, one_body):
    rotation = rotation_table(current.shape[2])
    both_sides = jnp.concatenate((propagator, jnp.swapaxes(propagator, 1, 2)), axis=2)
    term_now = current
    summed = current.astype(jnp.float32)
    for order_index in range(1, ORDER + 1):
        turned = jnp.einsum(
            "wqe,ef->wqf", term_now, rotation, preferred_element_type=jnp.float32
        ).astype(jnp.bfloat16)
        doubled = jnp.concatenate((turned, turned), axis=1)
        rotated = (
            jnp.einsum("wpq,wqe->wpe", both_sides, doubled, preferred_element_type=jnp.float32)
            / order_index
        )
        summed = summed + rotated
        term_now = rotated.astype(jnp.bfloat16)
    stepped = summed.astype(jnp.bfloat16)
    return jnp.einsum("pq,wqe->wpe", one_body, stepped, preferred_element_type=jnp.float32).astype(
        jnp.bfloat16
    )


def local(cholesky, fields, walkers, one_body):
    wide_count = lax.axis_size("wide")
    narrow_count = lax.axis_size("narrow")
    every_field = lax.all_gather(fields, "wide", axis=1, tiled=True)
    steps_total, walker_total, chol_rows = every_field.shape
    local_walkers, orbitals, columns = walkers.shape
    pair_cols = cholesky.shape[1]
    ordered = every_field.reshape(steps_total, wide_count, narrow_count, local_walkers, chol_rows)
    ordered = ordered.transpose(2, 0, 1, 3, 4).reshape(steps_total * walker_total, chol_rows)
    summed = lax.psum_scatter(
        jnp.dot(ordered, cholesky, preferred_element_type=jnp.float32).astype(jnp.bfloat16),
        "narrow",
        scatter_dimension=0,
        tiled=True,
    )
    tile_rows = summed.reshape(steps_total, wide_count, local_walkers, pair_cols)
    received = lax.all_to_all(tile_rows, "wide", split_axis=1, concat_axis=1, tiled=True)
    count_items = received.shape[0]
    propagators = received.transpose(0, 2, 1, 3).reshape(
        count_items, local_walkers, orbitals, orbitals
    )
    current = walkers
    for step_index in range(steps_total):
        current = advance(propagators[step_index], current, one_body)
    return current


def solution(mesh):
    return jax.shard_map(
        local,
        mesh=mesh,
        in_specs=(
            P("narrow", "wide"),
            P(None, "wide", "narrow"),
            P(("wide", "narrow"), None, None),
            P(),
        ),
        out_specs=P(("wide", "narrow"), None, None),
        check_vma=False,
    )
```

profile of v0, /device:TPU:0, one launch (start us, length us, event | category | flops | bytes accessed | tf_op | source)
XLA Modules:
  0.0 153.7 jit_solution(11601070356641359820)
XLA Ops:
  6.5 0.8 copy.26
  7.3 15.6 %all_gather.3 = bf16[2,32,512]{2,0,1:T(2,128)(2,1)S(1)} all-gather(bf16[2,4,512]{2,0,1:T(2,128)(2,1)S(1)} %copy.26), channel_id=1, replica_groups=mesh['wide'=8,'narrow'=4] {'wide'}, dimensions={1}, use_global_device_ids=true | all-gather | bytes 73728 | tf_op jit(solution)/shard_map/all_gather | solution.py:43
  23.0 18.4 %convolution_convert_fusion = bf16[64,32768]{1,0:T(8,128)(2,1)} fusion(bf16[64,512]{1,0:T(8,128)(2,1)S(1)} %bitcast.202, bf16[512,32768]{1,0:T(8,128)(2,1)} %param.4), kind=kOutput, calls=%fused_computation | convolution fusion | flops 2149580800 | bytes 37814272 | tf_op jit(solution)/shard_map/dot_general | solution.py:50
  41.4 53.9 %reduce-scatter.2.cloned.1.call-done = bf16[16,32768]{1,0:T(8,128)(2,1)} async-done(((bf16[64,32768]{1,0:T(8,128)(2,1)}), bf16[16,32768]{1,0:T(8,128)(2,1)}) %reduce-scatter.2.cloned.1.call-update) | async-done | bytes 1048592 | tf_op jit(solution)/shard_map/reduce_scatter | solution.py:49
  95.3 3.3 %copy.28 = bf16[2,8,1,32768]{3,0,2,1:T(2,128)(2,1)} copy(bf16[2,8,1,32768]{3,1,0,2:T(8,128)(2,1)} %bitcast.189) | data formatting | bytes 2097152 | tf_op jit(solution)/shard_map/reshape | solution.py:55
  98.6 4.6 %all-to-all-start = ((bf16[2,8,1,32768]{3,0,2,1:T(2,128)(2,1)}), bf16[2,8,1,32768]{3,0,2,1:T(2,128)(2,1)S(1)}, u32[]{:S(2)}, u32[]{:S(2)}) async-start(bf16[2,8,1,32768]{3,0,2,1:T(2,128)(2,1)} %copy.28), calls=%async_computation.1 | async-start | bytes 2097152 | tf_op jit(solution)/shard_map/all_to_all | solution.py:56
  103.3 0.2 fusion.7
  103.5 26.3 %all-to-all-done = bf16[2,8,1,32768]{3,0,2,1:T(2,128)(2,1)S(1)} async-done(((bf16[2,8,1,32768]{3,0,2,1:T(2,128)(2,1)}), bf16[2,8,1,32768]{3,0,2,1:T(2,128)(2,1)S(1)}, u32[]{:S(2)}, u32[]{:S(2)}) %all-to-all-start) | async-done | bytes 1048608 | tf_op jit(solution)/shard_map/all_to_all | solution.py:56
  129.8 4.5 %slice_reduce_fusion = (bf16[8,32768]{1,0:T(8,128)(2,1)S(1)}, bf16[8,32768]{1,0:T(8,128)(2,1)S(1)}) fusion(bf16[2,8,1,32768]{3,0,2,1:T(2,128)(2,1)S(1)} %all-to-all-done), kind=kLoop, calls=%fused_computation.46 | loop fusion | bytes 2097152 | tf_op jit(solution)/shard_map/slice | solution.py:63
  134.3 0.2 squeeze.7
  134.6 0.2 squeeze.6
  134.8 0.2 copy.29
  135.0 0.4 fusion.21
  135.5 0.2 fusion.8
  135.7 0.4 convolution_multiply_fusion.9
  136.3 0.4 convolution_multiply_fusion.8
  136.9 0.4 convolution_multiply_fusion.7
  137.4 0.2 fusion.11
  137.6 0.4 convolution_multiply_fusion.6
  138.0 0.2 fusion.12
  138.2 2.4 %convolution_convert_fusion.1 = bf16[128,512]{0,1:T(8,128)(2,1)} fusion(bf16[512,512]{1,0:T(8,128)(2,1)S(1)} %copy-done, bf16[1,512,128]{2,1,0:T(8,128)(2,1)S(1)} %fusion.12, f32[512,128]{1,0:T(8,128)S(1)} %convolution_multiply_fusion.6, f32[512,128]{1,0:T(8,128)S(1)} %convolution_multiply_fusion.7, f32[512,128]{1,0:T(8,128)S(1)} %convolution_multiply_fusion.8, ...), kind=kOutput, calls=%fused_computation.15 | convolution fusion | flops 204603392 | bytes 3276800 | tf_op jit(solution)/shard_map/pq,wqe->wpe/dot_general | solution.py:35
  140.7 1.1 fusion.13
  141.8 0.2 copy.31
  142.0 0.4 fusion.36
  142.4 0.2 fusion.14
  142.6 0.4 convolution_multiply_fusion.4
  143.2 0.4 convolution_multiply_fusion.3
  143.7 0.2 fusion.16
  143.9 0.4 convolution_multiply_fusion.2
  144.5 0.4 convolution_multiply_fusion.1
  145.2 0.9 fusion.6
  146.1 0.8 copy.32
  (16 shorter events, 1.1 us)
Async XLA Ops:
  6.5 131.7 %copy-start = (bf16[512,512]{1,0:T(8,128)(2,1)S(1)}, bf16[512,512]{1,0:T(8,128)(2,1)}, u32[]{:S(2)}) copy-start(bf16[512,512]{1,0:T(8,128)(2,1)} %param.7) | copy-start | bytes 1572868
  6.5 88.8 %reduce-scatter.2.cloned.1.call-start = ((), (), s32[]{:S(2)}) async-start(), calls=%async_computation.2 | async-start | bytes 5242880 | tf_op jit(solution)/shard_map/reduce_scatter | solution.py:49
  95.3 8.0 %copy-start.1 = (bf16[1,512,128]{2,1,0:T(8,128)(2,1)S(1)}, bf16[1,512,128]{2,1,0:T(8,128)(2,1)}, u32[]{:S(2)}) copy-start(bf16[1,512,128]{2,1,0:T(8,128)(2,1)} %param.6) | copy-start | bytes 393220
  98.6 31.2 %all-to-all-start = ((bf16[2,8,1,32768]{3,0,2,1:T(2,128)(2,1)}), bf16[2,8,1,32768]{3,0,2,1:T(2,128)(2,1)S(1)}, u32[]{:S(2)}, u32[]{:S(2)}) async-start(bf16[2,8,1,32768]{3,0,2,1:T(2,128)(2,1)} %copy.28), calls=%async_computation.1 | async-start | bytes 2097152 | tf_op jit(solution)/shard_map/all_to_all | solution.py:56
  144.3 0.9 copy-start.2
Sparse Core Ops, SparseCore 0:
  41.5 53.7 reduce-scatter.1
where the time goes:
time: 154 us
  waiting for transfers between devices  80.3 us (52%)
  matrix products  29.2 us (19%)
  blocking collectives  15.6 us (10%)
  between operations  13.6 us (9%)
  local copies, waits for them, and re-layouts  10.3 us (7%)
  starting transfers between devices  4.62 us (3%)
    reduce_scatter x1, waiting for transfers between devices, local(): lax.psum_scatter(jnp.dot(ordered, cholesky, preferred_element_type=jnp.fl...  53.9 us
    all_to_all x1, waiting for transfers between devices, local(): lax.all_to_all(tile_rows, 'wide', split_axis=1, concat_axis=1, tiled=True)  26.3 us
    dot_general x1, matrix products, local(): jnp.dot(ordered, cholesky, preferred_element_type=jnp.float32)  18.4 us
    all_gather x1, blocking collectives, local(): every_field = lax.all_gather(fields, 'wide', axis=1, tiled=True)  15.6 us
    all_to_all x1, starting transfers between devices, local(): lax.all_to_all(tile_rows, 'wide', split_axis=1, concat_axis=1, tiled=True)  4.62 us
    slice x1, local copies, waits for them, and re-layouts, local(): current = advance(propagators[step_index], current, one_body)  4.49 us
    dot_general x10, matrix products, advance(): jnp.einsum('wpq,wqe->wpe', both_sides, doubled, preferred_element_type=jn...  4.34 us
    dot_general x2, matrix products, advance(): jnp.einsum('pq,wqe->wpe', one_body, stepped, preferred_element_type=jnp.f...  3.32 us
  transfers between devices with their start and end apart: 2, of which 2 were waited for; matrix products, arithmetic and copies ran while one was open for 0% of the time, Pallas kernels for 0%

commit v1 on v0

--- a/solution.py
+++ b/solution.py
@@ -1,9 +1,15 @@
+import functools
+
 import jax
 import jax.numpy as jnp
 from jax import lax
+from jax.experimental import pallas as pl
+from jax.experimental.pallas import tpu as pltpu
 from jax.sharding import PartitionSpec as P
 
 ORDER = 6
+SUB = 8
+MIB = 1024 * 1024
 
 
 def rotation_table(columns):
@@ -37,7 +43,7 @@
     )
 
 
-def local(cholesky, fields, walkers, one_body):
+def general(cholesky, fields, walkers, one_body):
     wide_count = lax.axis_size("wide")
     narrow_count = lax.axis_size("narrow")
     every_field = lax.all_gather(fields, "wide", axis=1, tiled=True)
@@ -64,9 +70,245 @@
     return current
 
 
+def build_kernel(
+    wide, steps, orbitals, chunks,
+    fields_ref, chol_hbm, prop_ref,
+    chol, gathered, lhs, keep, send1, recv1, send2, recv2, fin32, fin16,
+    chol_sem, gs_sem, gr_sem, s1_sem, r1_sem, s2_sem, r2_sem, fs_sem, fr_sem,
+):
+    me = lax.axis_index("wide")
+    near = lax.axis_index("narrow")
+    row, col = lax.div(near, 2), lax.rem(near, 2)
+    across_x = row * 2 + (1 - col)
+    across_y = (1 - row) * 2 + col
+    cols = SUB * orbitals
+    group = steps * wide
+    blocks = chunks // 2
+    tile = 2 * orbitals
+
+    def chol_copy(k):
+        return pltpu.make_async_copy(
+            chol_hbm.at[:, pl.ds(k * cols, cols)], chol.at[k], chol_sem.at[k]
+        )
+
+    for k in range(chunks):
+        chol_copy(k).start()
+
+    def peer(d):
+        return lax.rem(me + d, wide)
+
+    barrier = pltpu.get_barrier_semaphore()
+    for d in range(1, wide):
+        pl.semaphore_signal(barrier, inc=1, device_id=(peer(d), near))
+    pl.semaphore_signal(barrier, inc=1, device_id=(me, across_x))
+    pl.semaphore_signal(barrier, inc=1, device_id=(me, across_y))
+    pl.semaphore_wait(barrier, wide + 1)
+
+    def field_copy(d):
+        return pltpu.make_async_remote_copy(
+            src_ref=fields_ref, dst_ref=gathered.at[me],
+            send_sem=gs_sem.at[d], recv_sem=gr_sem.at[d], device_id=(peer(d), near),
+        )
+
+    def field_arrival(d):
+        return pltpu.make_async_remote_copy(
+            src_ref=fields_ref, dst_ref=gathered.at[peer(wide - d)],
+            send_sem=gs_sem.at[d], recv_sem=gr_sem.at[d], device_id=(peer(d), near),
+        )
+
+    for d in range(1, wide):
+        field_copy(d).start()
+    gathered[me] = fields_ref[...]
+    for d in range(1, wide):
+        field_arrival(d).wait_recv()
+
+    for g in range(4):
+        rows = jnp.concatenate(
+            [gathered[:, g * steps + s, :] for s in range(steps)], axis=0
+        ).astype(jnp.bfloat16)
+        swapped = (0, 2, 1, 3)[g]
+        lhs[0, swapped * group:(swapped + 1) * group, :] = rows
+        lhs[1, g * group:(g + 1) * group, :] = rows
+
+    def first_copy(k):
+        return pltpu.make_async_remote_copy(
+            src_ref=send1.at[k], dst_ref=recv1.at[k], send_sem=s1_sem.at[k], recv_sem=r1_sem.at[k],
+            device_id=(me, across_x if k % 2 == 0 else across_y),
+        )
+
+    def second_copy(k):
+        return pltpu.make_async_remote_copy(
+            src_ref=send2.at[k], dst_ref=recv2.at[k], send_sem=s2_sem.at[k], recv_sem=r2_sem.at[k],
+            device_id=(me, across_y if k % 2 == 0 else across_x),
+        )
+
+    def multiply(k):
+        chol_copy(k).wait()
+
+        @pl.loop(0, cols // tile)
+        def _(i):
+            span = pl.ds(pl.multiple_of(i * tile, tile), tile)
+            part = jnp.dot(lhs[k % 2], chol[k, :, span], preferred_element_type=jnp.float32)
+            keep[k, :, span] = part[:2 * group]
+            send1[k, :, span] = part[2 * group:].astype(jnp.bfloat16)
+
+        first_copy(k).start()
+
+    def middle(k):
+        first_copy(k).wait_recv()
+
+        @pl.loop(0, cols // tile)
+        def _(i):
+            span = pl.ds(pl.multiple_of(i * tile, tile), tile)
+            part = keep[k, :, span] + recv1[k, :, span].astype(jnp.float32)
+            keep[k, :group, span] = part[:group]
+            send2[k, :, span] = part[group:].astype(jnp.bfloat16)
+
+        second_copy(k).start()
+
+    def last_copy(j, d):
+        return pltpu.make_async_remote_copy(
+            src_ref=fin16.at[j, peer(d)], dst_ref=prop_ref.at[:, me * blocks + j],
+            send_sem=fs_sem.at[j, d], recv_sem=fr_sem.at[j, d], device_id=(peer(d), near),
+        )
+
+    def last_arrival(j, d):
+        return pltpu.make_async_remote_copy(
+            src_ref=fin16.at[j, peer(d)], dst_ref=prop_ref.at[:, peer(wide - d) * blocks + j],
+            send_sem=fs_sem.at[j, d], recv_sem=fr_sem.at[j, d], device_id=(peer(d), near),
+        )
+
+    def finish(j):
+        for half in range(2):
+            k = 2 * j + half
+            second_copy(k).wait_recv()
+            for p in range(SUB):
+                span = pl.ds(p * orbitals, orbitals)
+                fin32[:, half * SUB + p, :] = (
+                    keep[k, :group, span] + recv2[k, :, span].astype(jnp.float32)
+                )
+        for s in range(steps):
+            for w in range(wide):
+                fin16[j, w, s] = fin32[s * wide + w].astype(jnp.bfloat16)
+        for d in range(1, wide):
+            last_copy(j, d).start()
+        prop_ref[:, me * blocks + j] = fin16[j, me]
+
+    for t in range(chunks + 5):
+        if t < chunks:
+            multiply(t)
+        if 0 <= t - 3 < chunks:
+            middle(t - 3)
+        if t - 5 >= 0 and (t - 5) % 2 == 1:
+            finish((t - 5) // 2)
+    for j in range(blocks):
+        for d in range(1, wide):
+            last_arrival(j, d).wait_recv()
+    for d in range(1, wide):
+        field_copy(d).wait_send()
+    for k in range(chunks):
+        first_copy(k).wait_send()
+        second_copy(k).wait_send()
+    for j in range(blocks):
+        for d in range(1, wide):
+            last_copy(j, d).wait_send()
+
+
+def taylor_kernel(steps, prop_ref, walker_ref, body_ref, out_ref):
+    columns = walker_ref.shape[1]
+    half_cols = columns // 2
+    lane = lax.broadcasted_iota(jnp.int32, (1, columns), 1)
+    sign = jnp.where(lane < half_cols, -1.0, 1.0).astype(jnp.float32)
+    sides = []
+    for s in range(steps):
+        wider = prop_ref[s].astype(jnp.float32)
+        sides.append((wider + wider.T).astype(jnp.bfloat16))
+    current = walker_ref[...]
+    for s in range(steps):
+        term_now = current
+        summed = current.astype(jnp.float32)
+        for order_index in range(1, ORDER + 1):
+            product = jnp.dot(sides[s], term_now, preferred_element_type=jnp.float32)
+            rotated = pltpu.roll(product, half_cols, 1) * (sign * (1.0 / order_index))
+            summed = summed + rotated
+            term_now = rotated.astype(jnp.bfloat16)
+        current = jnp.dot(
+            body_ref[...], summed.astype(jnp.bfloat16), preferred_element_type=jnp.float32
+        ).astype(jnp.bfloat16)
+    out_ref[...] = current
+
+
+def local(cholesky, fields, walkers, one_body):
+    wide = lax.axis_size("wide")
+    steps, _, depth = fields.shape
+    _, orbitals, columns = walkers.shape
+    pair_cols = cholesky.shape[1]
+    near = lax.axis_index("narrow")
+    row, col = near // 2, near % 2
+    grid = fields.astype(jnp.float32).reshape(steps, 2, 2, depth)
+    grid = jnp.where(row == 1, grid[:, ::-1], grid)
+    grid = jnp.where(col == 1, grid[:, :, ::-1], grid)
+    relative = grid.transpose(1, 2, 0, 3).reshape(4 * steps, depth)
+
+    chunk_cols = SUB * orbitals
+    chunks = pair_cols // chunk_cols
+    blocks = chunks // 2
+    group = steps * wide
+    vmem, dma = pltpu.VMEM, pltpu.SemaphoreType.DMA
+    bf16, f32 = jnp.bfloat16, jnp.float32
+    props = pl.pallas_call(
+        functools.partial(build_kernel, wide, steps, orbitals, chunks),
+        out_shape=jax.ShapeDtypeStruct((steps, wide * blocks, 2 * SUB, orbitals), bf16),
+        in_specs=[pl.BlockSpec(memory_space=pltpu.VMEM), pl.BlockSpec(memory_space=pl.ANY)],
+        out_specs=pl.BlockSpec(memory_space=pltpu.VMEM),
+        scratch_shapes=[
+            vmem((chunks, depth, chunk_cols), bf16),
+            vmem((wide, 4 * steps, depth), f32),
+            vmem((2, 4 * group, depth), bf16),
+            vmem((chunks, 2 * group, chunk_cols), f32),
+            vmem((chunks, 2 * group, chunk_cols), bf16),
+            vmem((chunks, 2 * group, chunk_cols), bf16),
+            vmem((chunks, group, chunk_cols), bf16),
+            vmem((chunks, group, chunk_cols), bf16),
+            vmem((group, 2 * SUB, orbitals), f32),
+            vmem((blocks, wide, steps, 2 * SUB, orbitals), bf16),
+            dma((chunks,)),
+            dma((wide,)), dma((wide,)),
+            dma((chunks,)), dma((chunks,)), dma((chunks,)), dma((chunks,)),
+            dma((blocks, wide)), dma((blocks, wide)),
+        ],
+        compiler_params=pltpu.CompilerParams(
+            collective_id=0, has_side_effects=True, vmem_limit_bytes=56 * MIB
+        ),
+        name="propagators",
+    )(relative, cholesky)
+    moved = pl.pallas_call(
+        functools.partial(taylor_kernel, steps),
+        out_shape=jax.ShapeDtypeStruct((orbitals, columns), bf16),
+        in_specs=[pl.BlockSpec(memory_space=pltpu.VMEM)] * 3,
+        out_specs=pl.BlockSpec(memory_space=pltpu.VMEM),
+        compiler_params=pltpu.CompilerParams(vmem_limit_bytes=32 * MIB),
+        name="taylor",
+    )(props.reshape(steps, orbitals, orbitals), walkers[0], one_body)
+    return moved[None]
+
+
 def solution(mesh):
+    def choose(cholesky, fields, walkers, one_body):
+        _, orbitals, _ = walkers.shape
+        pair_cols = cholesky.shape[1]
+        group = fields.shape[0] * lax.axis_size("wide")
+        fits = (
+            lax.axis_size("narrow") == 4
+            and walkers.shape[0] == 1
+            and group % 16 == 0
+            and pair_cols % (2 * SUB * orbitals) == 0
+            and cholesky.shape[0] * pair_cols * 2 <= 32 * MIB
+        )
+        return (local if fits else general)(cholesky, fields, walkers, one_body)
+
     return jax.shard_map(
-        local,
+        choose,
         mesh=mesh,
         in_specs=(
             P("narrow", "wide"),

time: 154 us -> 70.4 us (0.46)
  waiting for transfers between devices: 80.3 us -> 0 us
  Pallas kernels: 0 us -> 67.4 us
  matrix products: 29.2 us -> 0 us
  blocking collectives: 15.6 us -> 0 us
  between operations: 13.6 us -> 0.05 us
  local copies, waits for them, and re-layouts: 10.3 us -> 2.61 us
  starting transfers between devices: 4.62 us -> 0 us
    pallas_call x0 -> x2, Pallas kernels: none -> 67.4 us  [the longest x1 61.2 us: local(): pl.pallas_call(functools.partial(build_kernel, wide, steps, orbitals, chu...]
    reduce_scatter x1 -> x0, waiting for transfers between devices: 53.9 us -> none  [local(): lax.psum_scatter(jnp.dot(ordered, cholesky, preferred_element_type=jnp.fl...]
    dot_general x25 -> x0, matrix products: 29.2 us -> none  [the longest x1 18.4 us: local(): jnp.dot(ordered, cholesky, preferred_element_type=jnp.float32)]
    all_to_all x1 -> x0, waiting for transfers between devices: 26.3 us -> none  [local(): lax.all_to_all(tile_rows, 'wide', split_axis=1, concat_axis=1, tiled=True)]
    all_gather x1 -> x0, blocking collectives: 15.6 us -> none  [local(): every_field = lax.all_gather(fields, 'wide', axis=1, tiled=True)]
    all_to_all x1 -> x0, starting transfers between devices: 4.62 us -> none  [local(): lax.all_to_all(tile_rows, 'wide', split_axis=1, concat_axis=1, tiled=True)]
    slice x1 -> x0, local copies, waits for them, and re-layouts: 4.49 us -> none  [local(): current = advance(propagators[step_index], current, one_body)]
    reshape x1 -> x2, local copies, waits for them, and re-layouts: 3.31 us -> 1.39 us  [the longest x1 0.77 us: local(): grid = fields.astype(jnp.float32).reshape(steps, 2, 2, depth)]
  transfers between devices with their start and end apart: 2 -> 0, of which waited for: 2 -> 0; matrix products, arithmetic and copies ran while one was open for 0% -> 0% of each run, Pallas kernels for 0% -> 0%
where the time goes in v1:
time: 70.4 us; the launch traced here: 70.1 us
  Pallas kernels  67.4 us (96%)
  local copies, waits for them, and re-layouts  2.61 us (4%)
    pallas_call x1, Pallas kernels, local(): pl.pallas_call(functools.partial(build_kernel, wide, steps, orbitals, chu...  61.2 us
    pallas_call x1, Pallas kernels, local(): pl.pallas_call(functools.partial(taylor_kernel, steps), out_shape=jax.Sha...  6.18 us

profile of v1, /device:TPU:0, one launch (start us, length us, event | category | flops | bytes accessed | tf_op | source)
XLA Modules:
  0.0 70.1 jit_solution(15075150204095475699)
XLA Ops:
  0.0 0.0 copy-start.1
  0.0 0.0 copy-start.2
  0.0 0.8 %copy.7 = f32[2,4,512]{2,0,1:T(2,128)S(1)} copy(bf16[2,4,512]{2,1,0:T(4,128)(2,1)} %param.5) | data formatting | bytes 24576 | tf_op jit(solution)/shard_map/reshape | solution.py:248
  0.8 0.6 reshape.14.fields_ref
  1.4 61.2 %propagators.1 = bf16[2,32,16,512]{3,2,1,0:T(8,128)(2,1)} custom-call(f32[8,512]{1,0:T(8,128)} %reshape.14.fields_ref, bf16[512,32768]{1,0:T(8,128)(2,1)} %chol_hbm.1), custom_call_target="tpu_custom_call" | custom-call | tf_op jit(solution)/shard_map/propagators/pallas_call | solution.py:259
  62.7 0.0 copy-done.1
  62.7 0.0 copy-done.2
  62.7 0.0 copy-start
  62.7 1.2 %copy-done = bf16[2,32,16,512]{3,2,1,0:T(8,128)(2,1)S(1)} copy-done((bf16[2,32,16,512]{3,2,1,0:T(8,128)(2,1)S(1)}, bf16[2,32,16,512]{3,2,1,0:T(8,128)(2,1)}, u32[]{:S(2)}) %copy-start) | copy-done | bytes 1048600
  63.9 6.2 %taylor.1 = bf16[512,128]{1,0:T(8,128)(2,1)} custom-call(bf16[2,512,512]{2,1,0:T(8,128)(2,1)S(1)} %bitcast.6, bf16[512,128]{1,0:T(8,128)(2,1)S(1)} %bitcast.7, bf16[512,512]{1,0:T(8,128)(2,1)S(1)} %copy-done.1), custom_call_target="tpu_custom_call" | custom-call | tf_op jit(solution)/shard_map/taylor/pallas_call | solution.py:285
  (2 shorter events, 0.0 us)
Async XLA Ops:
  0.0 62.7 %copy-start.1 = (bf16[512,512]{1,0:T(8,128)(2,1)S(1)}, bf16[512,512]{1,0:T(8,128)(2,1)}, u32[]{:S(2)}) copy-start(bf16[512,512]{1,0:T(8,128)(2,1)} %body_ref.1) | copy-start | bytes 1572868
  0.0 62.7 %copy-start.2 = (bf16[1,512,128]{2,1,0:T(8,128)(2,1)S(1)}, bf16[1,512,128]{2,1,0:T(8,128)(2,1)}, u32[]{:S(2)}) copy-start(bf16[1,512,128]{2,1,0:T(8,128)(2,1)} %param.6) | copy-start | bytes 393220
  62.7 1.2 %copy-start = (bf16[2,32,16,512]{3,2,1,0:T(8,128)(2,1)S(1)}, bf16[2,32,16,512]{3,2,1,0:T(8,128)(2,1)}, u32[]{:S(2)}) copy-start(bf16[2,32,16,512]{3,2,1,0:T(8,128)(2,1)} %propagators.1) | copy-start | bytes 3145732

commit v2 on v0

--- a/solution.py
+++ b/solution.py
@@ -1,9 +1,15 @@
+import functools
+
 import jax
 import jax.numpy as jnp
 from jax import lax
+from jax.experimental import pallas as pl
+from jax.experimental.pallas import tpu as pltpu
 from jax.sharding import PartitionSpec as P
 
 ORDER = 6
+SUB = 8
+MIB = 1024 * 1024
 
 
 def rotation_table(columns):
@@ -37,7 +43,7 @@
     )
 
 
-def local(cholesky, fields, walkers, one_body):
+def general(cholesky, fields, walkers, one_body):
     wide_count = lax.axis_size("wide")
     narrow_count = lax.axis_size("narrow")
     every_field = lax.all_gather(fields, "wide", axis=1, tiled=True)
@@ -64,9 +70,277 @@
     return current
 
 
+def propagate_kernel(
+    wide, steps, orbitals, chunks,
+    fields_ref, chol_hbm, walker_ref, body_ref, out_ref,
+    chol, own, gathered, lhs, keep, send1, recv1, send2, recv2, fin32, fin16, prop,
+    chol_sem, gs_sem, gr_sem, s1_sem, r1_sem, s2_sem, r2_sem, fs_sem, fr_sem,
+):
+    me = lax.axis_index("wide")
+    near = lax.axis_index("narrow")
+    row, col = lax.div(near, 2), lax.rem(near, 2)
+    across_x = row * 2 + (1 - col)
+    across_y = (1 - row) * 2 + col
+    cols = SUB * orbitals
+    both = 2 * wide
+    blocks = chunks // 2
+    tile = 2 * orbitals
+    ahead = 3
+
+    def chol_copy(k):
+        return pltpu.make_async_copy(
+            chol_hbm.at[:, pl.ds(k * cols, cols)], chol.at[k], chol_sem.at[k]
+        )
+
+    for k in range(min(ahead, chunks)):
+        chol_copy(k).start()
+
+    def peer(d):
+        return lax.rem(me + d, wide)
+
+    barrier = pltpu.get_barrier_semaphore()
+    for d in range(1, wide):
+        pl.semaphore_signal(barrier, inc=1, device_id=(peer(d), near))
+    pl.semaphore_signal(barrier, inc=1, device_id=(me, across_x))
+    pl.semaphore_signal(barrier, inc=1, device_id=(me, across_y))
+
+    mine = fields_ref[...].astype(jnp.float32)
+    for s in range(steps):
+        for a in range(2):
+            for b in range(2):
+                def pick(y, x):
+                    return mine[s, 2 * y + x:2 * y + x + 1, :]
+
+                upper = jnp.where(col == 0, pick(a, b), pick(a, 1 - b))
+                lower = jnp.where(col == 0, pick(1 - a, b), pick(1 - a, 1 - b))
+                at = (2 * a + b) * steps + s
+                own[at:at + 1, :] = jnp.where(row == 0, upper, lower)
+    pl.semaphore_wait(barrier, wide + 1)
+
+    def field_copy(d, source):
+        return pltpu.make_async_remote_copy(
+            src_ref=own, dst_ref=gathered.at[source],
+            send_sem=gs_sem.at[d], recv_sem=gr_sem.at[d], device_id=(peer(d), near),
+        )
+
+    for d in range(1, wide):
+        field_copy(d, me).start()
+    for k in range(ahead, min(ahead + 2, chunks)):
+        chol_copy(k).start()
+    gathered[me] = own[...]
+    for d in range(1, wide):
+        field_copy(d, peer(wide - d)).wait_recv()
+
+    for path, order in enumerate(((0, 2, 1, 3), (0, 1, 2, 3))):
+        for role in range(2):
+            first, second = order[2 * role:2 * role + 2]
+            for s in range(steps):
+                at = (role * steps + s) * both
+                lhs[path, at:at + both, :] = jnp.concatenate(
+                    [gathered[:, first * steps + s, :], gathered[:, second * steps + s, :]], axis=0
+                ).astype(jnp.bfloat16)
+
+    def first_copy(s, k):
+        return pltpu.make_async_remote_copy(
+            src_ref=send1.at[s, k], dst_ref=recv1.at[s, k],
+            send_sem=s1_sem.at[s, k], recv_sem=r1_sem.at[s, k],
+            device_id=(me, across_x if k % 2 == 0 else across_y),
+        )
+
+    def second_copy(s, k):
+        return pltpu.make_async_remote_copy(
+            src_ref=send2.at[s, k], dst_ref=recv2.at[s, k],
+            send_sem=s2_sem.at[s, k], recv_sem=r2_sem.at[s, k],
+            device_id=(me, across_y if k % 2 == 0 else across_x),
+        )
+
+    def multiply(k):
+        chol_copy(k).wait()
+        if k + ahead + 2 < chunks:
+            chol_copy(k + ahead + 2).start()
+
+        @pl.loop(0, cols // tile)
+        def _(i):
+            span = pl.ds(pl.multiple_of(i * tile, tile), tile)
+            part = jnp.dot(lhs[k % 2], chol[k, :, span], preferred_element_type=jnp.float32)
+            for s in range(steps):
+                keep[s, k, :, span] = part[s * both:(s + 1) * both]
+                send1[s, k, :, span] = part[
+                    (steps + s) * both:(steps + s + 1) * both
+                ].astype(jnp.bfloat16)
+
+    def middle(s, k):
+        first_copy(s, k).wait_recv()
+
+        @pl.loop(0, cols // (2 * tile))
+        def _(i):
+            outgoing = []
+            for half in range(2):
+                start = pl.multiple_of(half * (cols // 2) + i * tile, tile)
+                span = pl.ds(start, tile)
+                part = keep[s, k, :, span] + recv1[s, k, :, span].astype(jnp.float32)
+                keep[s, k, :wide, span] = part[:wide]
+                outgoing.append(part[wide:])
+            span = pl.ds(pl.multiple_of(i * tile, tile), tile)
+            send2[s, k, :, span] = jnp.concatenate(outgoing, axis=0).astype(jnp.bfloat16)
+
+        second_copy(s, k).start()
+
+    def last_copy(s, j, d, source):
+        return pltpu.make_async_remote_copy(
+            src_ref=fin16.at[s, j, peer(d)], dst_ref=prop.at[s, source * blocks + j],
+            send_sem=fs_sem.at[s, j, d], recv_sem=fr_sem.at[s, j, d], device_id=(peer(d), near),
+        )
+
+    def finish(s, j):
+        for half in range(2):
+            k = 2 * j + half
+            second_copy(s, k).wait_recv()
+            for p in range(SUB // 2):
+                later = p + SUB // 2
+                span = pl.ds(p * orbitals, orbitals)
+                arrived = recv2[s, k, :, span].astype(jnp.float32)
+                fin32[:, half * SUB + p, :] = keep[s, k, :wide, span] + arrived[:wide]
+                fin32[:, half * SUB + later, :] = (
+                    keep[s, k, :wide, pl.ds(later * orbitals, orbitals)] + arrived[wide:]
+                )
+        for w in range(wide):
+            fin16[s, j, w] = fin32[w].astype(jnp.bfloat16)
+        for d in range(1, wide):
+            last_copy(s, j, d, me).start()
+        prop[s, me * blocks + j] = fin16[s, j, me]
+
+    columns = walker_ref.shape[1]
+    half_cols = columns // 2
+    lane = lax.broadcasted_iota(jnp.int32, (1, columns), 1)
+    sign = jnp.where(lane < half_cols, -1.0, 1.0).astype(jnp.float32)
+
+    def taylor(s):
+        for j in range(blocks):
+            for d in range(1, wide):
+                last_copy(s, j, d, peer(wide - d)).wait_recv()
+        wider = prop[s].reshape(orbitals, orbitals).astype(jnp.float32)
+        sides = (wider + wider.T).astype(jnp.bfloat16)
+        term_now = walker_ref[...] if s == 0 else out_ref[...]
+        summed = term_now.astype(jnp.float32)
+        for order_index in range(1, ORDER + 1):
+            product = jnp.dot(sides, term_now, preferred_element_type=jnp.float32)
+            rotated = pltpu.roll(product, half_cols, 1) * (sign * (1.0 / order_index))
+            summed = summed + rotated
+            term_now = rotated.astype(jnp.bfloat16)
+        out_ref[...] = jnp.dot(
+            body_ref[...], summed.astype(jnp.bfloat16), preferred_element_type=jnp.float32
+        ).astype(jnp.bfloat16)
+
+    early = 2
+    finished = 0
+    for k in range(chunks):
+        multiply(k)
+        for s in range(steps if k < early else 1):
+            first_copy(s, k).start()
+        if k >= 3:
+            middle(0, k - 3)
+        if k >= 6 and k % 2 == 0:
+            finish(0, finished)
+            finished += 1
+    waiting = [(s, k) for s in range(1, steps) for k in range(early, chunks)]
+    for k in range(max(chunks - 3, 0), chunks):
+        for held in waiting[:2]:
+            first_copy(*held).start()
+        waiting = waiting[2:]
+        middle(0, k)
+    for held in waiting:
+        first_copy(*held).start()
+    for s in range(1, steps):
+        for k in range(early):
+            middle(s, k)
+    for j in range(finished, blocks):
+        finish(0, j)
+    for s in range(1, steps):
+        finished = 0
+        for k in range(early, chunks):
+            if k == chunks - 2:
+                taylor(s - 1)
+            middle(s, k)
+            if k % 2 == 1:
+                finish(s, finished)
+                finished += 1
+        if chunks <= early:
+            taylor(s - 1)
+        for j in range(finished, blocks):
+            finish(s, j)
+    taylor(steps - 1)
+
+    for d in range(1, wide):
+        field_copy(d, me).wait_send()
+    for s in range(steps):
+        for k in range(chunks):
+            first_copy(s, k).wait_send()
+            second_copy(s, k).wait_send()
+        for j in range(blocks):
+            for d in range(1, wide):
+                last_copy(s, j, d, me).wait_send()
+
+
+def local(cholesky, fields, walkers, one_body):
+    wide = lax.axis_size("wide")
+    steps, _, depth = fields.shape
+    _, orbitals, columns = walkers.shape
+    chunk_cols = SUB * orbitals
+    chunks = cholesky.shape[1] // chunk_cols
+    blocks = chunks // 2
+    both = 2 * wide
+    vmem, dma = pltpu.VMEM, pltpu.SemaphoreType.DMA
+    bf16, f32 = jnp.bfloat16, jnp.float32
+    in_vmem = pl.BlockSpec(memory_space=pltpu.VMEM)
+    moved = pl.pallas_call(
+        functools.partial(propagate_kernel, wide, steps, orbitals, chunks),
+        out_shape=jax.ShapeDtypeStruct((orbitals, columns), bf16),
+        in_specs=[in_vmem, pl.BlockSpec(memory_space=pl.ANY), in_vmem, in_vmem],
+        out_specs=in_vmem,
+        scratch_shapes=[
+            vmem((chunks, depth, chunk_cols), bf16),
+            vmem((4 * steps, depth), f32),
+            vmem((wide, 4 * steps, depth), f32),
+            vmem((2, 2 * steps * both, depth), bf16),
+            vmem((steps, chunks, both, chunk_cols), f32),
+            vmem((steps, chunks, both, chunk_cols), bf16),
+            vmem((steps, chunks, both, chunk_cols), bf16),
+            vmem((steps, chunks, both, chunk_cols // 2), bf16),
+            vmem((steps, chunks, both, chunk_cols // 2), bf16),
+            vmem((wide, 2 * SUB, orbitals), f32),
+            vmem((steps, blocks, wide, 2 * SUB, orbitals), bf16),
+            vmem((steps, wide * blocks, 2 * SUB, orbitals), bf16),
+            dma((chunks,)),
+            dma((wide,)), dma((wide,)),
+            dma((steps, chunks)), dma((steps, chunks)),
+            dma((steps, chunks)), dma((steps, chunks)),
+            dma((steps, blocks, wide)), dma((steps, blocks, wide)),
+        ],
+        compiler_params=pltpu.CompilerParams(
+            collective_id=0, has_side_effects=True, vmem_limit_bytes=58 * MIB
+        ),
+        name="propagate",
+    )(fields, cholesky, walkers[0], one_body)
+    return moved[None]
+
+
 def solution(mesh):
+    def choose(cholesky, fields, walkers, one_body):
+        _, orbitals, _ = walkers.shape
+        pair_cols = cholesky.shape[1]
+        both = 2 * lax.axis_size("wide")
+        fits = (
+            lax.axis_size("narrow") == 4
+            and walkers.shape[0] == 1
+            and both % 16 == 0
+            and pair_cols % (2 * SUB * orbitals) == 0
+            and cholesky.shape[0] * pair_cols * 2 <= 32 * MIB
+        )
+        return (local if fits else general)(cholesky, fields, walkers, one_body)
+
     return jax.shard_map(
-        local,
+        choose,
         mesh=mesh,
         in_specs=(
             P("narrow", "wide"),

time: 154 us -> 66.2 us (0.43)
  waiting for transfers between devices: 80.3 us -> 0 us
  Pallas kernels: 0 us -> 64.5 us
  matrix products: 29.2 us -> 0 us
  blocking collectives: 15.6 us -> 0 us
  between operations: 13.6 us -> 0.01 us
  local copies, waits for them, and re-layouts: 10.3 us -> 1.57 us
  starting transfers between devices: 4.62 us -> 0 us
    pallas_call x0 -> x1, Pallas kernels: none -> 64.5 us  [local(): pl.pallas_call(functools.partial(propagate_kernel, wide, steps, orbitals,...]
    reduce_scatter x1 -> x0, waiting for transfers between devices: 53.9 us -> none  [local(): lax.psum_scatter(jnp.dot(ordered, cholesky, preferred_element_type=jnp.fl...]
    dot_general x25 -> x0, matrix products: 29.2 us -> none  [the longest x1 18.4 us: local(): jnp.dot(ordered, cholesky, preferred_element_type=jnp.float32)]
    all_to_all x1 -> x0, waiting for transfers between devices: 26.3 us -> none  [local(): lax.all_to_all(tile_rows, 'wide', split_axis=1, concat_axis=1, tiled=True)]
    all_gather x1 -> x0, blocking collectives: 15.6 us -> none  [local(): every_field = lax.all_gather(fields, 'wide', axis=1, tiled=True)]
    all_to_all x1 -> x0, starting transfers between devices: 4.62 us -> none  [local(): lax.all_to_all(tile_rows, 'wide', split_axis=1, concat_axis=1, tiled=True)]
    slice x1 -> x0, local copies, waits for them, and re-layouts: 4.49 us -> none  [local(): current = advance(propagators[step_index], current, one_body)]
    reshape x1 -> x0, local copies, waits for them, and re-layouts: 3.31 us -> none  [local(): summed.reshape(steps_total, wide_count, local_walkers, pair_cols)]
  transfers between devices with their start and end apart: 2 -> 0, of which waited for: 2 -> 0; matrix products, arithmetic and copies ran while one was open for 0% -> 0% of each run, Pallas kernels for 0% -> 0%
where the time goes in v2:
time: 66.2 us; the launch traced here: 66.1 us
  Pallas kernels  64.5 us (97%)
  local copies, waits for them, and re-layouts  1.57 us (2%)
    pallas_call x1, Pallas kernels, local(): pl.pallas_call(functools.partial(propagate_kernel, wide, steps, orbitals,...  64.5 us
    unnamed x1, local copies, waits for them, and re-layouts  1.57 us

profile of v2, /device:TPU:0, one launch (start us, length us, event | category | flops | bytes accessed | tf_op | source)
XLA Modules:
  0.0 66.1 jit_solution(14738492811860634149)
XLA Ops:
  0.0 64.5 %propagate.1 = bf16[512,128]{1,0:T(8,128)(2,1)} custom-call(bf16[2,4,512]{2,1,0:T(4,128)(2,1)} %fields_ref.1, bf16[512,32768]{1,0:T(8,128)(2,1)} %chol_hbm.1, bf16[512,128]{1,0:T(8,128)(2,1)} %bitcast.3, bf16[512,512]{1,0:T(8,128)(2,1)} %body_ref.1), custom_call_target="tpu_custom_call" | custom-call | tf_op jit(solution)/shard_map/propagate/pallas_call | solution.py:296
  64.5 1.6 %copy.6 = bf16[1,512,128]{2,1,0:T(8,128)(2,1)} copy(bf16[1,512,128]{2,1,0:T(8,128)(2,1)} %bitcast.2) | data formatting | bytes 262144

commit v3 on v2

--- a/solution.py
+++ b/solution.py
@@ -232,7 +232,7 @@
             body_ref[...], summed.astype(jnp.bfloat16), preferred_element_type=jnp.float32
         ).astype(jnp.bfloat16)
 
-    early = 2
+    early = max(chunks - 2, 0)
     finished = 0
     for k in range(chunks):
         multiply(k)
@@ -243,32 +243,35 @@
         if k >= 6 and k % 2 == 0:
             finish(0, finished)
             finished += 1
-    waiting = [(s, k) for s in range(1, steps) for k in range(early, chunks)]
-    for k in range(max(chunks - 3, 0), chunks):
-        for held in waiting[:2]:
-            first_copy(*held).start()
-        waiting = waiting[2:]
+    for s in range(1, steps):
+        for k in range(early, chunks):
+            first_copy(s, k).start()
+    coming = [(1, k) for k in range(chunks)] if steps > 1 else []
+
+    def take(count):
+        for item in coming[:count]:
+            middle(*item)
+        del coming[:count]
+
+    for i, k in enumerate(range(max(chunks - 3, 0), chunks)):
         middle(0, k)
-    for held in waiting:
-        first_copy(*held).start()
+        take(2 if i == 0 else 1)
+    if finished < blocks - 1:
+        finish(0, finished)
+        finished += 1
+    take(len(coming) - 1)
+    for j in range(finished, blocks - 1):
+        finish(0, j)
+    take(len(coming))
+    finish(0, blocks - 1)
     for s in range(1, steps):
-        for k in range(early):
-            middle(s, k)
-    for j in range(finished, blocks):
-        finish(0, j)
-    for s in range(1, steps):
-        finished = 0
-        for k in range(early, chunks):
-            if k == chunks - 2:
-                taylor(s - 1)
-            middle(s, k)
-            if k % 2 == 1:
-                finish(s, finished)
-                finished += 1
-        if chunks <= early:
-            taylor(s - 1)
-        for j in range(finished, blocks):
+        if s > 1:
+            for k in range(chunks):
+                middle(s, k)
+        for j in range(blocks - 1):
             finish(s, j)
+        taylor(s - 1)
+        finish(s, blocks - 1)
     taylor(steps - 1)
 
     for d in range(1, wide):

time: 66.2 us -> 67.7 us (1.023)
  Pallas kernels: 64.5 us -> 66 us
    pallas_call x1, Pallas kernels: 64.5 us -> 66 us  [local(): pl.pallas_call(functools.partial(propagate_kernel, wide, steps, orbitals,...]
where the time goes in v3:
time: 67.7 us; the launch traced here: 67.6 us
  Pallas kernels  66 us (97%)
  local copies, waits for them, and re-layouts  1.57 us (2%)
    pallas_call x1, Pallas kernels, local(): pl.pallas_call(functools.partial(propagate_kernel, wide, steps, orbitals,...  66 us
    unnamed x1, local copies, waits for them, and re-layouts  1.57 us

profile of v3, /device:TPU:0, one launch (start us, length us, event | category | flops | bytes accessed | tf_op | source)
XLA Modules:
  0.0 67.6 jit_solution(5864919645390807010)
XLA Ops:
  0.0 66.0 %propagate.1 = bf16[512,128]{1,0:T(8,128)(2,1)} custom-call(bf16[2,4,512]{2,1,0:T(4,128)(2,1)} %fields_ref.1, bf16[512,32768]{1,0:T(8,128)(2,1)} %chol_hbm.1, bf16[512,128]{1,0:T(8,128)(2,1)} %bitcast.3, bf16[512,512]{1,0:T(8,128)(2,1)} %body_ref.1), custom_call_target="tpu_custom_call" | custom-call | tf_op jit(solution)/shard_map/propagate/pallas_call | solution.py:299
  66.0 1.6 %copy.6 = bf16[1,512,128]{2,1,0:T(8,128)(2,1)} copy(bf16[1,512,128]{2,1,0:T(8,128)(2,1)} %bitcast.2) | data formatting | bytes 262144
